TPU v7x, 32 devices: a whole 2x2x4 slice. The times are simulated.
32 devices in a mesh: groups: 2 (over y), seq: 4 (over z), head: 2 (over x), sub: 2 (over core).
Axes of the slice: x: 2, y: 2, z: 4, core: 2. Of those that a mesh axis runs over, the one named last changes fastest.
Arguments:
- queries: bfloat16 [8192, 2048], P(('groups', 'seq', 'sub'), 'head'), parts along dimension 0, may hold values from -4.5 to 4.5
- keys: bfloat16 [8192, 2048], P(('groups', 'seq', 'sub'), 'head'), parts along dimension 0, may hold values from -4.5 to 4.5
- values: bfloat16 [8192, 2048], P(('groups', 'seq', 'sub'), 'head'), parts along dimension 0, may hold values from -6 to 6
- grad_out: bfloat16 [8192, 2048], P(('groups', 'seq', 'sub'), 'head'), parts along dimension 0, may hold values from -6 to 6
- cluster_ids: int32 [16, 8192, 1], P('head', ('groups', 'seq', 'sub')), parts along dimension 1, may hold values from 0 to 63; in each aligned block of 512 rows (0 to 511, 512 to 1023, ..., all dimensions but the last counted through in order) at most 12 rows name the same one
Outputs:
- attention: bfloat16 [8192, 2048], P(('groups', 'seq', 'sub'), 'head'), parts along dimension 0
- grad_queries: bfloat16 [8192, 2048], P(('groups', 'seq', 'sub'), 'head'), parts along dimension 0
- grad_keys: bfloat16 [8192, 2048], P(('groups', 'seq', 'sub'), 'head'), parts along dimension 0
- grad_values: bfloat16 [8192, 2048], P(('groups', 'seq', 'sub'), 'head'), parts along dimension 0
- centroid_sums: float32 [16, 128, 128], P('head', 'groups'), parts along dimension 1
There are 2 independent parts, one for each index of `groups`. A program takes and returns all parts, laid end to end along the dimension named above; each array names one. Nothing has to cross between parts.
Inputs may be any that keep to these rules, and one draw needn't show every extreme that they name: `cluster_ids`: in each head, the tokens of one device (aligned blocks of 512 tokens) name one cluster at most 12 times, a bound that some block reaches.
All inputs are finite; a program needn't handle non-finite values.
Results may differ from a plain program's by a relative error of at most 0.0052.
Values may be sent and summed in bfloat16 or wider, within the bound.
A program may use at most 128 MiB of HBM per device.

v0:
```python
import functools
import jax
import jax.numpy as jnp
from jax import lax
from jax.experimental import pallas as pl
from jax.experimental.pallas import tpu as pltpu
from jax.sharding import PartitionSpec as P

CLUSTERS = 64
CAP = 12
SLOT = 16
AXES = ("seq", "sub")
VMEM = 56 * 1024 * 1024


norm_eps = 1e-06
masked_score = -1e30


def unit_rows(matrix):
    return matrix * lax.rsqrt(jnp.sum(matrix * matrix, axis=-1, keepdims=True) + norm_eps)


def cluster_work(packed, counts):
    head_width = packed.shape[-1] // 4
    row_count = packed.shape[2]
    slot_rank = (jnp.arange(row_count) % CAP).astype(jnp.float32)
    filled = jnp.repeat(counts.astype(jnp.float32), CAP, axis=2)
    filled_slot = slot_rank[None, None, :] < filled
    query_rows = packed[..., :head_width]
    key_rows = packed[..., head_width : 2 * head_width]
    value_rows = packed[..., 2 * head_width : 3 * head_width]
    grad_rows = packed[..., 3 * head_width :]
    score_scale = head_width ** (-0.5)
    scores = (
        jnp.einsum("hcqd,hckd->hcqk", query_rows, key_rows, preferred_element_type=jnp.float32)
        * score_scale
    )
    scores = jnp.where(filled_slot[:, :, None, :], scores, masked_score)
    row_max = jnp.max(scores, axis=-1, keepdims=True)
    exp_scores = jnp.exp(scores - row_max)
    probabilities = exp_scores / jnp.sum(exp_scores, axis=-1, keepdims=True)
    weights = probabilities.astype(jnp.bfloat16)
    attention = jnp.einsum(
        "hcqk,hckd->hcqd", weights, value_rows, preferred_element_type=jnp.float32
    ).astype(jnp.bfloat16)
    dprobs = jnp.einsum(
        "hcqd,hckd->hcqk", grad_rows, value_rows, preferred_element_type=jnp.float32
    )
    row_delta = jnp.sum(probabilities * dprobs, axis=-1, keepdims=True)
    dscore = (score_scale * probabilities * (dprobs - row_delta)).astype(jnp.bfloat16)
    dquery = jnp.einsum(
        "hcqk,hckd->hcqd", dscore, key_rows, preferred_element_type=jnp.float32
    ).astype(jnp.bfloat16)
    dkey = jnp.einsum(
        "hcqk,hcqd->hckd", dscore, query_rows, preferred_element_type=jnp.float32
    ).astype(jnp.bfloat16)
    dvalue = jnp.einsum(
        "hcqk,hcqd->hckd", weights, grad_rows, preferred_element_type=jnp.float32
    ).astype(jnp.bfloat16)
    result = jnp.concatenate([attention, dquery, dkey, dvalue], axis=-1)
    cluster_sums = None
    return (result, cluster_sums)


def padded_path(queries, keys, values, grad_out, cluster_ids):
    tok_rows = queries.shape[0]
    heads_here = cluster_ids.shape[0]
    head_width = queries.shape[1] // heads_here
    cluster_of = cluster_ids[:, :, 0]
    member = (
        cluster_of[:, :, None] == jnp.arange(CLUSTERS, dtype=jnp.int32)[None, None, :]
    ).astype(jnp.int32)
    before = jnp.cumsum(member, axis=1) - member
    slot_rank = jnp.sum(before * member, axis=2)
    slot_index = cluster_of * CAP + slot_rank
    dispatch = (
        slot_index[:, None, :] == jnp.arange(CLUSTERS * CAP, dtype=jnp.int32)[None, :, None]
    ).astype(jnp.bfloat16)
    counts = jnp.sum(member, axis=1).astype(jnp.bfloat16)[:, :, None]
    head_shape = (tok_rows, heads_here, head_width)
    stacked = jnp.stack(
        [
            queries.reshape(head_shape),
            keys.reshape(head_shape),
            values.reshape(head_shape),
            grad_out.reshape(head_shape),
        ],
        axis=2,
    )
    packed = jnp.einsum(
        "hst,thfd->hsfd", dispatch, stacked, preferred_element_type=jnp.float32
    ).astype(jnp.bfloat16)
    packed = packed.reshape(heads_here, CLUSTERS, CAP, 4 * head_width)
    result, _ = cluster_work(
        lax.all_to_all(packed, AXES, split_axis=1, concat_axis=2, tiled=True),
        lax.all_to_all(counts, AXES, split_axis=1, concat_axis=2, tiled=True),
    )
    sent_back = lax.all_to_all(result, AXES, split_axis=2, concat_axis=1, tiled=True)
    rows_back = sent_back.reshape(heads_here, CLUSTERS * CAP, 4, head_width)
    merged = jnp.einsum(
        "hst,hsfd->thfd", dispatch, rows_back, preferred_element_type=jnp.float32
    ).astype(jnp.bfloat16)
    flat_shape = (tok_rows, heads_here * head_width)
    return tuple(merged[:, :, i, :].reshape(flat_shape) for i in range(4))


def up16(x):
    return -(-x // 16) * 16


def one_hot(hit):
    return jnp.where(hit, 1.0, 0.0).astype(jnp.bfloat16)


def dot(a, b, ca=1, cb=0):
    return lax.dot_general(
        a, b, (((ca,), (cb,)), ((), ())), preferred_element_type=jnp.float32
    )


def exchange_kernel(n, sub, hc, chunks, width, window, room,
                    q_ref, k_ref, v_ref, g_ref, pos_ref, tgt_ref, cnt_ref,
                    out_a, out_q, out_k, out_v, tails_ref,
                    send, recv, ret, back, win, x, r, from_row, filled, send_sem, recv_sem):
    outs = (out_a, out_q, out_k, out_v)
    tokens = q_ref.shape[0]
    blocks = hc * (CLUSTERS // n)
    slots = blocks * SLOT
    scale = width ** (-0.5)
    iota = functools.partial(lax.broadcasted_iota, jnp.int32)
    me = lax.axis_index("seq") * sub + lax.axis_index("sub")

    def peer(o):
        return {"seq": o // sub, "sub": o % sub}

    def loop(first, last, body):
        lax.fori_loop(first, last, lambda i, carry: (body(i), carry)[1], 0)

    def ahead(d):
        return lax.rem(me + d, n)

    def behind(d):
        return lax.rem(me + n - d, n)

    def copy(way, c, there, mine):
        source, target = ((send, recv), (ret, back))[way]
        return pltpu.make_async_remote_copy(
            src_ref=source.at[c, there],
            dst_ref=target.at[c, mine],
            send_sem=send_sem.at[way, c, there],
            recv_sem=recv_sem.at[way, c, mine],
            device_id=peer(there),
            device_id_type=pl.DeviceIdType.MESH,
        )

    def launch(way, c, earlier):
        def one(d):
            o = ahead(d)
            if earlier is not None:
                copy(*earlier, o, me).wait_send()
            copy(way, c, o, me).start()

        loop(1, n, one)

    def arrived(way, c, d):
        copy(way, c, ahead(d), behind(d)).wait_recv()

    def pack(c):
        slot = iota((n * window, tokens), 0)
        for h in range(hc):
            at = (c * hc + h) * width
            cols = slice(at, at + width)
            rows = jnp.concatenate(
                [q_ref[:, cols], k_ref[:, cols], v_ref[:, cols], g_ref[:, cols]], axis=1
            )
            got = dot(one_hot(slot == pos_ref[c * hc + h]), rows).astype(jnp.bfloat16)
            win[:, h * window:(h + 1) * window, :] = got.reshape(n, window, 4 * width)
        place = iota((room, hc * window), 0)
        last = iota((room, 4 * width), 0) == room - 1

        def rows_for(o):
            rows = dot(one_hot(place == tgt_ref[c, o]), win[o])
            return jnp.where(last, cnt_ref[c, o], rows).astype(jnp.bfloat16)

        def to_owner(d):
            o = ahead(d)
            send[c, o] = rows_for(o)
            if c == 0:
                copy(0, c, o, me).start()

        loop(1, n, to_owner)
        recv[c, me] = rows_for(me)

    def work(c):
        sublane = iota((room, slots), 0)
        tails = recv[c, :, room - 16:, :128]
        if c == 0:
            tails_ref[...] = tails
        tails = tails.reshape(n * 16, 128)
        lane, block = iota((128, slots), 0), iota((128, slots), 1) // SLOT
        count = dot(tails, one_hot(lane == block))
        first = dot(tails, one_hot(lane < block))
        rank = (iota((n * 16, slots), 1) % SLOT).astype(jnp.float32)
        from_row[...] = jnp.where(rank < count, first + rank, -1.0).reshape(n, 16, slots)
        shape = (n * 16, n * SLOT)
        tail_of = one_hot(iota(shape, 0) == iota(shape, 1) // SLOT * 16 + 15)
        per_block = dot(tails, tail_of, 0, 0)
        rank = (iota((128, n * SLOT), 1) % SLOT).astype(jnp.float32)
        filled[...] = jnp.where(rank < per_block, 1.0, 0.0)

        def places(s):
            return one_hot(sublane.astype(jnp.float32) == from_row[s, 15:16, :])

        def take(s):
            got = dot(places(s), recv[c, s], 0, 0).astype(jnp.bfloat16)
            at = pl.ds(pl.multiple_of(s * SLOT, SLOT), SLOT)
            x[:, at, :] = got.reshape(blocks, SLOT, 4 * width)

        loop(0, n, take)

        def one(i):
            q = x[i, :, :width]
            k = x[i, :, width:2 * width]
            v = x[i, :, 2 * width:3 * width]
            g = x[i, :, 3 * width:]
            scores = dot(q, k, 1, 1) * scale
            scores = jnp.where(filled[pl.ds(i, 1), :] > 0, scores, masked_score)
            e = jnp.exp(scores - jnp.max(scores, axis=-1, keepdims=True))
            p = e / jnp.sum(e, axis=-1, keepdims=True)
            w = p.astype(jnp.bfloat16)
            dp = dot(g, v, 1, 1)
            delta = jnp.sum(p * dp, axis=-1, keepdims=True)
            ds = (scale * p * (dp - delta)).astype(jnp.bfloat16)
            r[i, :, :width] = dot(w, v).astype(jnp.bfloat16)
            r[i, :, width:2 * width] = dot(ds, k).astype(jnp.bfloat16)
            r[i, :, 2 * width:3 * width] = dot(ds, q, 0, 0).astype(jnp.bfloat16)
            r[i, :, 3 * width:] = dot(w, g, 0, 0).astype(jnp.bfloat16)

        step = 4 if blocks % 4 == 0 and n * SLOT <= 256 else 1

        def attend(i):
            for j in range(step):
                one(i * step + j)

        loop(0, blocks // step, attend)

        def rows_for(s):
            at = pl.ds(pl.multiple_of(s * SLOT, SLOT), SLOT)
            rows = r[:, at, :].reshape(slots, 4 * width)
            return dot(places(s), rows).astype(jnp.bfloat16)

        def give(d):
            s = ahead(d)
            ret[c, s] = rows_for(s)

        loop(1, n, give)
        back[c, me] = rows_for(me)

    def unpack(c):
        place = iota((room, hc * window), 0)

        def fill(o):
            hit = one_hot(place == tgt_ref[c, o])
            win[o] = dot(hit, back[c, o], 0, 0).astype(jnp.bfloat16)

        def from_owner(d):
            arrived(1, c, d)
            fill(behind(d))

        fill(me)
        loop(1, n, from_owner)
        slot = iota((n * window, tokens), 0)
        for h in range(hc):
            rows = win[:, h * window:(h + 1) * window, :].reshape(n * window, 4 * width)
            got = dot(one_hot(slot == pos_ref[c * hc + h]), rows, 0, 0).astype(jnp.bfloat16)
            at = (c * hc + h) * width
            for f in range(4):
                outs[f][:, at:at + width] = got[:, f * width:(f + 1) * width]

    barrier = pltpu.get_barrier_semaphore()
    loop(1, n, lambda d: pl.semaphore_signal(
        barrier, inc=1, device_id=peer(ahead(d)), device_id_type=pl.DeviceIdType.MESH
    ))
    pl.semaphore_wait(barrier, n - 1)
    pack(0)
    under_way = (0, 0)
    for c in range(1, chunks):
        pack(c)
        launch(0, c, under_way)
        under_way = (0, c)
    for c in range(chunks):
        loop(1, n, functools.partial(arrived, 0, c))
        work(c)
        launch(1, c, under_way)
        under_way = (1, c)
    for c in range(chunks):
        unpack(c)
    loop(1, n, lambda d: copy(*under_way, ahead(d), me).wait_send())


def shards(n, sub, queries, keys, values, grad_out, cluster_ids):
    tok_rows = queries.shape[0]
    heads = cluster_ids.shape[0]
    width = queries.shape[1] // heads
    k = CLUSTERS // n
    chunks = 2 if heads % 2 == 0 else 1
    hc = heads // chunks
    window = up16(k * CAP)
    room = up16(hc * k * CAP * 5 // 6)
    blocks = hc * k
    four = 4 * width
    params = pltpu.CompilerParams(vmem_limit_bytes=VMEM)

    cl = cluster_ids[:, :, 0]
    head_no = jnp.arange(heads, dtype=jnp.int32)[:, None]
    minor = cl // n
    owner = (cl % n + head_no * minor) % n
    cid = owner * k + minor
    names = jnp.arange(CLUSTERS, dtype=jnp.int32)
    member = (cid[:, :, None] == names).astype(jnp.bfloat16)
    tok = jnp.arange(tok_rows)
    earlier = (tok[:, None] > tok[None, :]).astype(jnp.bfloat16)
    before = jnp.einsum("ts,hsc->htc", earlier, member, preferred_element_type=jnp.float32)
    counts = jnp.sum(member.astype(jnp.float32), axis=1)
    same = (names[:, None] // k == names[None, :] // k) & (names[:, None] < names[None, :])
    start = jnp.sum(counts[:, :, None] * same.astype(jnp.float32), axis=1)
    start = start + (names // k * window).astype(jnp.float32)
    pos = jnp.sum(member.astype(jnp.float32) * (before + start[:, None, :]), axis=2)
    pos = pos.astype(jnp.int32)
    seg = jnp.sum(counts.reshape(chunks, hc, n, k), axis=3).astype(jnp.int32)
    ends = jnp.cumsum(seg, axis=1)
    base = ends - seg
    overflow = (jnp.max(ends) > room - 1).astype(jnp.float32)
    j = jnp.arange(window, dtype=jnp.int32)
    tgt = jnp.where(j < seg[..., None], base[..., None] + j, -1)
    tgt = jnp.swapaxes(tgt, 1, 2).reshape(chunks, n, hc * window)
    cnt_row = jnp.swapaxes(counts.reshape(chunks, hc, n, k), 1, 2).reshape(chunks, n, 1, blocks)
    flag = jnp.broadcast_to(overflow, (chunks, n, 1, 1))
    rest = jnp.zeros((chunks, n, 1, four - blocks - 1), jnp.float32)
    cnt_row = jnp.concatenate([cnt_row, flag, rest], axis=3)

    normed = unit_rows(keys.reshape(tok_rows, heads, width).astype(jnp.float32))
    own = (cl[:, :, None] == names).astype(jnp.float32)
    partial_sums = jnp.einsum("htc,thd->hcd", own, normed, precision=lax.Precision.HIGHEST)
    centroid_sums = lax.psum(partial_sums, AXES)
    wide = jax.ShapeDtypeStruct((tok_rows, heads * width), jnp.bfloat16)
    slots = blocks * SLOT
    parcel = pltpu.VMEM((chunks, n, room, four), jnp.bfloat16)
    *outs, tails = pl.pallas_call(
        functools.partial(exchange_kernel, n, sub, hc, chunks, width, window, room),
        out_shape=[wide] * 4 + [jax.ShapeDtypeStruct((n, 16, 128), jnp.bfloat16)],
        in_specs=[pl.BlockSpec(memory_space=pltpu.VMEM)] * 7,
        out_specs=[pl.BlockSpec(memory_space=pltpu.VMEM)] * 5,
        scratch_shapes=[parcel] * 4
        + [
            pltpu.VMEM((n, hc * window, four), jnp.bfloat16),
            pltpu.VMEM((blocks, n * SLOT, four), jnp.bfloat16),
            pltpu.VMEM((blocks, n * SLOT, four), jnp.bfloat16),
            pltpu.VMEM((n, 16, slots), jnp.float32),
            pltpu.VMEM((128, n * SLOT), jnp.float32),
            pltpu.SemaphoreType.DMA((2, chunks, n)),
            pltpu.SemaphoreType.DMA((2, chunks, n)),
        ],
        compiler_params=pltpu.CompilerParams(
            vmem_limit_bytes=VMEM, collective_id=0, has_side_effects=True
        ),
        cost_estimate=pl.CostEstimate(flops=5 * 10**10, bytes_accessed=10**7, transcendentals=10**6),
    )(queries, keys, values, grad_out, pos[:, None, :], tgt[:, :, None, :], cnt_row)
    outs = lax.cond(
        jnp.max(tails[:, 15, blocks]) > 0,
        lambda: padded_path(queries, keys, values, grad_out, cluster_ids),
        lambda: tuple(outs),
    )
    return (*outs, centroid_sums)


def solution(mesh):
    n = mesh.shape["seq"] * mesh.shape["sub"]
    rows = P(("groups", "seq", "sub"), "head")
    return jax.shard_map(
        functools.partial(shards, n, mesh.shape["sub"]),
        mesh=mesh,
        in_specs=(rows, rows, rows, rows, P("head", ("groups", "seq", "sub"), None)),
        out_specs=(rows, rows, rows, rows, P("head", "groups", None)),
        check_vma=False,
    )
```

profile of v0, /device:TPU:1, one launch (start us, length us, event | category | flops | bytes accessed | tf_op | source)
XLA Modules:
  0.0 277.5 jit_solution(6164834099360829381)
XLA Ops:
  7.2 1.5 convert_bitcast_fusion.2
  8.7 0.5 copy.243
  9.2 0.6 multiply_reduce_fusion.1
  9.8 0.6 broadcast_multiply_fusion
  10.5 1.9 fusion.50
  12.4 0.2 fusion.64
  12.6 0.2 convert_reduce_fusion.1
  12.8 0.1 reduce_sum.84
  13.2 0.1 add.122
  13.5 0.1 lt.87
  13.7 0.6 reduce_max.27
  15.3 0.1 multiply_reduce_fusion.2
  15.5 0.6 fusion.54
  16.1 0.6 convert_element_type.139.pos_ref
  16.7 0.6 compare_select_fusion.tgt_ref
  17.3 0.6 maximum_maximum_fusion.cnt_ref
  18.0 243.0 %shard_map.92 = (bf16[512,1024]{1,0:T(8,128)(2,1)}, bf16[512,1024]{1,0:T(8,128)(2,1)}, bf16[512,1024]{1,0:T(8,128)(2,1)}, bf16[512,1024]{1,0:T(8,128)(2,1)}, bf16[8,16,128]{2,1,0:T(8,128)(2,1)}) custom-call(bf16[512,1024]{1,0:T(8,128)(2,1)S(1)} %copy-done.1, bf16[512,1024]{1,0:T(8,128)(2,1)S(1)} %copy-done, bf16[512,1024]{1,0:T(8,128)(2,1)S(1)} %copy-done.3, ...), custom_call_target="tpu_custom_call" | custom-call | flops 49999998976 | bytes 10000000 | tf_op jit(solution)/shard_map/pallas_call | solution.py:350
  260.9 1.4 slice_reduce_fusion
  263.0 0.3 conditional.1
  263.3 2.4 copy.293
  265.7 2.3 copy.294
  268.0 1.0 copy.295
  269.0 1.0 copy.296
  270.0 0.7 copy.297
  (40 shorter events, 1.1 us)
Async XLA Ops:
  7.2 256.1 %all-reduce.2.cloned.1.call-start = ((), (), s32[]{:S(2)}) async-start(), calls=%async_computation.3 | async-start | bytes 524288 | tf_op jit(solution)/shard_map/psum | solution.py:346
  9.2 1.3 copy-start.9
  10.5 7.5 %copy-start = (bf16[512,1024]{1,0:T(8,128)(2,1)S(1)}, bf16[512,1024]{1,0:T(8,128)(2,1)}, u32[]{:S(2)}) copy-start(bf16[512,1024]{1,0:T(8,128)(2,1)} %k_ref.1) | copy-start | bytes 3145732
  10.5 7.5 %copy-start.1 = (bf16[512,1024]{1,0:T(8,128)(2,1)S(1)}, bf16[512,1024]{1,0:T(8,128)(2,1)}, u32[]{:S(2)}) copy-start(bf16[512,1024]{1,0:T(8,128)(2,1)} %q_ref.1) | copy-start | bytes 3145732
  10.5 7.5 %copy-start.3 = (bf16[512,1024]{1,0:T(8,128)(2,1)S(1)}, bf16[512,1024]{1,0:T(8,128)(2,1)}, u32[]{:S(2)}) copy-start(bf16[512,1024]{1,0:T(8,128)(2,1)} %v_ref.1) | copy-start | bytes 3145732
  263.3 4.8 %copy-start.8 = (bf16[512,1024]{1,0:T(8,128)(2,1)S(1)}, bf16[512,1024]{1,0:T(8,128)(2,1)}, u32[]{:S(2)}) copy-start(bf16[512,1024]{1,0:T(8,128)(2,1)} %get-tuple-element.167) | copy-start | bytes 3145732
  263.3 5.7 %copy-start.7 = (bf16[512,1024]{1,0:T(8,128)(2,1)S(1)}, bf16[512,1024]{1,0:T(8,128)(2,1)}, u32[]{:S(2)}) copy-start(bf16[512,1024]{1,0:T(8,128)(2,1)} %get-tuple-element.168) | copy-start | bytes 3145732
  265.7 4.3 %copy-start.10 = (f32[8,64,128]{2,1,0:T(8,128)S(1)}, f32[8,64,128]{2,1,0:T(8,128)}, u32[]{:S(2)}) copy-start(f32[8,64,128]{2,1,0:T(8,128)} %all-reduce.2.cloned.1.call-done) | copy-start | bytes 786436
Sparse Core Ops, SparseCore 0:
  12.5 166.4 all-reduce.1
where the time goes:
time: 278 us
  Pallas kernels  243 us (87%)
  between operations  15.6 us (6%)
  local copies, waits for them, and re-layouts  9.48 us (3%)
  other arithmetic  6.78 us (2%)
    pallas_call x1, Pallas kernels, shards(): pl.pallas_call(functools.partial(exchange_kernel, n, sub, hc, chunks, wid...  243 us
    unnamed x22, local copies, waits for them, and re-layouts  7.86 us
  transfers between devices with their start and end apart: 1, of which 0 were waited for; matrix products, arithmetic and copies ran while one was open for 2% of the time, Pallas kernels for 88%

commit v1 on v0

--- a/solution.py
+++ b/solution.py
@@ -137,11 +137,14 @@
     def loop(first, last, body):
         lax.fori_loop(first, last, lambda i, carry: (body(i), carry)[1], 0)
 
+    def turn(d):
+        return lax.rem(d + n // 2 - 2 + (n - 1), n - 1) + 1
+
     def ahead(d):
-        return lax.rem(me + d, n)
+        return lax.rem(me + turn(d), n)
 
     def behind(d):
-        return lax.rem(me + n - d, n)
+        return lax.rem(me + n - turn(d), n)
 
     def copy(way, c, there, mine):
         source, target = ((send, recv), (ret, back))[way]

time: 278 us -> 279 us (level)
  the two profiles are of different devices: /device:TPU:1 before, /device:TPU:0 now
where the time goes in v1:
time: 279 us; the launch traced here: 278 us
  Pallas kernels  244 us (87%)
  between operations  15.6 us (6%)
  local copies, waits for them, and re-layouts  9.48 us (3%)
  other arithmetic  6.78 us (2%)
    pallas_call x1, Pallas kernels, shards(): pl.pallas_call(functools.partial(exchange_kernel, n, sub, hc, chunks, wid...  244 us
    unnamed x22, local copies, waits for them, and re-layouts  7.86 us
  transfers between devices with their start and end apart: 1, of which 0 were waited for; matrix products, arithmetic and copies ran while one was open for 2% of the time, Pallas kernels for 88%

profile of v1, /device:TPU:0, one launch (start us, length us, event | category | flops | bytes accessed | tf_op | source)
XLA Modules:
  0.0 278.3 jit_solution(14147545903969456615)
XLA Ops:
  7.2 1.5 convert_bitcast_fusion.2
  8.7 0.5 copy.243
  9.2 0.6 multiply_reduce_fusion.1
  9.8 0.6 broadcast_multiply_fusion
  10.5 1.9 fusion.50
  12.4 0.2 fusion.64
  12.6 0.2 convert_reduce_fusion.1
  12.8 0.1 reduce_sum.84
  13.2 0.1 add.122
  13.5 0.1 lt.87
  13.7 0.6 reduce_max.27
  15.3 0.1 multiply_reduce_fusion.2
  15.5 0.6 fusion.54
  16.1 0.6 convert_element_type.139.pos_ref
  16.7 0.6 compare_select_fusion.tgt_ref
  17.3 0.6 maximum_maximum_fusion.cnt_ref
  18.0 243.7 %shard_map.92 = (bf16[512,1024]{1,0:T(8,128)(2,1)}, bf16[512,1024]{1,0:T(8,128)(2,1)}, bf16[512,1024]{1,0:T(8,128)(2,1)}, bf16[512,1024]{1,0:T(8,128)(2,1)}, bf16[8,16,128]{2,1,0:T(8,128)(2,1)}) custom-call(bf16[512,1024]{1,0:T(8,128)(2,1)S(1)} %copy-done.1, bf16[512,1024]{1,0:T(8,128)(2,1)S(1)} %copy-done, bf16[512,1024]{1,0:T(8,128)(2,1)S(1)} %copy-done.3, ...), custom_call_target="tpu_custom_call" | custom-call | flops 49999998976 | bytes 10000000 | tf_op jit(solution)/shard_map/pallas_call | solution.py:353
  261.7 1.4 slice_reduce_fusion
  263.7 0.3 conditional.1
  264.0 2.4 copy.293
  266.4 2.3 copy.294
  268.8 1.0 copy.295
  269.7 1.0 copy.296
  270.7 0.7 copy.297
  (40 shorter events, 1.1 us)
Async XLA Ops:
  7.2 256.9 %all-reduce.2.cloned.1.call-start = ((), (), s32[]{:S(2)}) async-start(), calls=%async_computation.3 | async-start | bytes 524288 | tf_op jit(solution)/shard_map/psum | solution.py:349
  9.2 1.3 copy-start.9
  10.5 7.5 %copy-start = (bf16[512,1024]{1,0:T(8,128)(2,1)S(1)}, bf16[512,1024]{1,0:T(8,128)(2,1)}, u32[]{:S(2)}) copy-start(bf16[512,1024]{1,0:T(8,128)(2,1)} %k_ref.1) | copy-start | bytes 3145732
  10.5 7.5 %copy-start.1 = (bf16[512,1024]{1,0:T(8,128)(2,1)S(1)}, bf16[512,1024]{1,0:T(8,128)(2,1)}, u32[]{:S(2)}) copy-start(bf16[512,1024]{1,0:T(8,128)(2,1)} %q_ref.1) | copy-start | bytes 3145732
  10.5 7.5 %copy-start.3 = (bf16[512,1024]{1,0:T(8,128)(2,1)S(1)}, bf16[512,1024]{1,0:T(8,128)(2,1)}, u32[]{:S(2)}) copy-start(bf16[512,1024]{1,0:T(8,128)(2,1)} %v_ref.1) | copy-start | bytes 3145732
  264.0 4.8 %copy-start.8 = (bf16[512,1024]{1,0:T(8,128)(2,1)S(1)}, bf16[512,1024]{1,0:T(8,128)(2,1)}, u32[]{:S(2)}) copy-start(bf16[512,1024]{1,0:T(8,128)(2,1)} %get-tuple-element.167) | copy-start | bytes 3145732
  264.0 5.7 %copy-start.7 = (bf16[512,1024]{1,0:T(8,128)(2,1)S(1)}, bf16[512,1024]{1,0:T(8,128)(2,1)}, u32[]{:S(2)}) copy-start(bf16[512,1024]{1,0:T(8,128)(2,1)} %get-tuple-element.168) | copy-start | bytes 3145732
  266.4 4.3 %copy-start.10 = (f32[8,64,128]{2,1,0:T(8,128)S(1)}, f32[8,64,128]{2,1,0:T(8,128)}, u32[]{:S(2)}) copy-start(f32[8,64,128]{2,1,0:T(8,128)} %all-reduce.2.cloned.1.call-done) | copy-start | bytes 786436
Sparse Core Ops, SparseCore 0:
  12.5 115.3 all-reduce.1
